TPU v7x, 1024 devices: a whole 4x8x16 slice. The times are simulated.
1024 devices in a mesh: own: 32 (over z_lo, x, core), grp: 32 (over y, z_hi).
Axes of the slice: x: 4, y: 8, z: 16 (z_hi: 4, z_lo: 4; z = z_hi * 4 + z_lo), core: 2. Of those that a mesh axis runs over, the one named last changes fastest.
Arguments:
- tokens: bfloat16 [4096, 2048], P('own'), may hold values from -6 to 6
- cotangent: bfloat16 [4096, 2048], P('own'), may hold values from -6 to 6
- route_ids: int32 [4096, 6], P('own'), may hold values from 0 to 63, all different within a row; in each aligned block of 128 rows (0 to 127, 128 to 255, ...) at most 15 rows name the same one
- route_weights: float32 [4096, 6], P('own'), may hold values from 0.1 to 1
- gate_weight: bfloat16 [1024, 512, 352], P(('own', 'grp')), may hold values from -0.125 to 0.125
- up_weight: bfloat16 [1024, 512, 352], P(('own', 'grp')), may hold values from -0.125 to 0.125
- down_weight_t: bfloat16 [1024, 512, 352], P(('own', 'grp')), may hold values from -0.15625 to 0.15625
Outputs:
- layer_out: bfloat16 [4096, 2048], P('own', 'grp')
- token_grad: bfloat16 [4096, 2048], P('own', 'grp')
- gate_grad: float32 [1024, 512, 352], P(('own', 'grp'))
- up_grad: float32 [1024, 512, 352], P(('own', 'grp'))
- down_grad: float32 [1024, 512, 352], P(('own', 'grp'))
Inputs may be any that keep to these rules, and one draw needn't show every extreme that they name: `route_ids`: each row names 6 different experts. In each aligned block of 128 rows (the rows of one index of own) no expert is named by more than 15 rows, a bound that some block reaches.
All inputs are finite; a program needn't handle non-finite values.
Results may differ from a plain program's by a relative error of at most 0.0064.
Values may be sent and summed in bfloat16 or wider, within the bound.
A program may use at most 32 MiB of HBM per device.

v0:
```python
import jax
import jax.numpy as jnp
from jax import lax
from jax.sharding import PartitionSpec as P

D = 2048
FF = 1408
EXP_DEV = 2


def partner(block, axis, bit):
    count = lax.axis_size(axis)
    route = []
    for low in range(count):
        high = low | 1 << bit
        if high != low and high < count:
            route += [(low, high), (high, low)]
    return lax.ppermute(block, axis, route)


def silu_value(gating, up_proj):
    sigmoid_gate = jax.nn.sigmoid(gating)
    return (gating * sigmoid_gate * up_proj).astype(jnp.bfloat16)


def silu_grads(grad_hidden, gating, up_proj):
    sigmoid_gate = jax.nn.sigmoid(gating)
    grad_gate = (
        grad_hidden * up_proj * sigmoid_gate * (1.0 + gating * (1.0 - sigmoid_gate))
    ).astype(jnp.bfloat16)
    grad_up = (grad_hidden * gating * sigmoid_gate).astype(jnp.bfloat16)
    return (grad_gate, grad_up)


def on_device(tokens, cotangent, route_ids, route_weights, gate_weight, up_weight, down_weight_t):
    owners = lax.axis_size("own")
    grp_index = lax.axis_index("grp")
    tok_dev, top_count = route_ids.shape
    block_width = gate_weight.shape[1]
    slice_width = gate_weight.shape[2]
    d_split = D // block_width
    f_split = FF // slice_width
    low_count = EXP_DEV * f_split
    experts = EXP_DEV * owners
    capacity = max(2, min(tok_dev, 5 * tok_dev * top_count // (4 * experts)))
    d_block = grp_index // low_count
    expert_bit = grp_index // f_split % EXP_DEV
    route_total = tok_dev * top_count
    row_total = owners * capacity
    routes = route_ids.reshape(route_total)
    onehot = (routes[:, None] == jnp.arange(experts, dtype=jnp.int32)[None, :]).astype(jnp.int32)
    before = jnp.cumsum(onehot, axis=0) - onehot
    position = jnp.sum(before * onehot, axis=1)
    is_mine = routes % EXP_DEV == expert_bit
    target = jnp.where(is_mine, routes // EXP_DEV * capacity + position, row_total)
    token_of = jnp.arange(route_total, dtype=jnp.int32) // top_count
    flat_weights = route_weights.reshape(route_total)
    row_token = jnp.zeros((row_total,), jnp.int32).at[target].set(token_of, mode="drop")
    row_weight = jnp.zeros((row_total,), jnp.float32).at[target].set(flat_weights, mode="drop")
    row_used = (
        jnp.zeros((row_total,), jnp.bfloat16)
        .at[target]
        .set(jnp.ones((route_total,), jnp.bfloat16), mode="drop")
    )
    tok_part = lax.dynamic_slice_in_dim(tokens, d_block * block_width, block_width, 1)
    cot_part = lax.dynamic_slice_in_dim(cotangent, d_block * block_width, block_width, 1)
    sent_inputs = tok_part[row_token] * row_used[:, None]
    sent_cots = (row_weight[:, None] * cot_part[row_token].astype(jnp.float32)).astype(jnp.bfloat16)
    shape_out = (owners, capacity, block_width)
    got_inputs, got_cots = (
        lax.all_to_all(
            sent_inputs.reshape(shape_out), "own", split_axis=0, concat_axis=0, tiled=True
        ),
        lax.all_to_all(
            sent_cots.reshape(shape_out), "own", split_axis=0, concat_axis=0, tiled=True
        ),
    )
    inputs = got_inputs.reshape(row_total, block_width)
    cotangents = got_cots.reshape(row_total, block_width)
    w_gate = gate_weight[0]
    w_up = up_weight[0]
    w_down = down_weight_t[0]
    part_gate = jnp.dot(inputs, w_gate, preferred_element_type=jnp.float32)
    part_up = jnp.dot(inputs, w_up, preferred_element_type=jnp.float32)
    part_grad = jnp.dot(cotangents, w_down, preferred_element_type=jnp.float32)
    base_bit = low_count.bit_length() - 1
    d_bits = [base_bit + offset for offset in range(d_split.bit_length() - 1)]
    summed = jnp.stack([part_gate, part_up, part_grad])
    for bit_pos in d_bits:
        summed = summed + partner(summed, "grp", bit_pos)
    hidden = silu_value(summed[0], summed[1])
    grad_gate, grad_up = silu_grads(summed[2], summed[0], summed[1])
    out_part = jnp.einsum("rf,df->rd", hidden, w_down, preferred_element_type=jnp.float32).astype(
        jnp.bfloat16
    )
    grad_part = (
        jnp.einsum("rf,df->rd", grad_gate, w_gate, preferred_element_type=jnp.float32)
        + jnp.einsum("rf,df->rd", grad_up, w_up, preferred_element_type=jnp.float32)
    ).astype(jnp.bfloat16)
    gate_grad = jnp.einsum("rd,rf->df", inputs, grad_gate, preferred_element_type=jnp.float32)[None]
    up_grad = jnp.einsum("rd,rf->df", inputs, grad_up, preferred_element_type=jnp.float32)[None]
    down_grad = jnp.einsum("rd,rf->df", cotangents, hidden, preferred_element_type=jnp.float32)[
        None
    ]
    back_out, back_grad = (
        lax.all_to_all(out_part.reshape(shape_out), "own", split_axis=0, concat_axis=0, tiled=True),
        lax.all_to_all(
            grad_part.reshape(shape_out), "own", split_axis=0, concat_axis=0, tiled=True
        ),
    )
    back_rows = back_out.reshape(row_total, block_width)
    grad_rows = back_grad.reshape(row_total, block_width)
    safe_target = jnp.minimum(target, row_total - 1)
    mine_mask = is_mine.astype(jnp.float32)
    picked_out = back_rows[safe_target].astype(jnp.float32) * (flat_weights * mine_mask)[:, None]
    picked_grad = grad_rows[safe_target].astype(jnp.float32) * mine_mask[:, None]
    layer_part = jnp.sum(picked_out.reshape(tok_dev, top_count, block_width), axis=1)
    token_part = jnp.sum(picked_grad.reshape(tok_dev, top_count, block_width), axis=1)
    gathered = jnp.stack([layer_part, token_part])
    for bit_pos in reversed(range(base_bit)):
        half_cols = gathered.shape[2] // 2
        bit_on = grp_index // 2**bit_pos % 2 == 1
        lower_half = gathered[:, :, :half_cols]
        upper_half = gathered[:, :, half_cols:]
        kept_half = jnp.where(bit_on, upper_half, lower_half)
        sent_half = jnp.where(bit_on, lower_half, upper_half)
        gathered = kept_half + partner(sent_half, "grp", bit_pos)
    layer_out = gathered[0].astype(jnp.bfloat16)
    token_grad = gathered[1].astype(jnp.bfloat16)
    return (layer_out, token_grad, gate_grad, up_grad, down_grad)


def solution(mesh):
    placed = (
        P("own", None),
        P("own", None),
        P("own", None),
        P("own", None),
        P(("own", "grp"), None, None),
        P(("own", "grp"), None, None),
        P(("own", "grp"), None, None),
    )
    return jax.shard_map(
        on_device,
        mesh=mesh,
        in_specs=placed,
        out_specs=(
            P("own", "grp"),
            P("own", "grp"),
            P(("own", "grp"), None, None),
            P(("own", "grp"), None, None),
            P(("own", "grp"), None, None),
        ),
        check_vma=False,
    )
```

profile of v0, /device:TPU:4, one launch (start us, length us, event | category | flops | bytes accessed | tf_op | source)
XLA Modules:
  0.0 376.3 jit_solution(16924457012881699478)
XLA Ops:
  0.7 0.8 copy.21
  1.8 0.1 reshape.260
  2.0 1.8 reduce-window.6
  3.8 0.3 slice_reduce_fusion
  4.1 0.1 fusion.17
  4.3 3.4 scatter_custom_fusion
  7.7 1.0 constant_dynamic-slice_fusion
  8.7 2.1 gather_fusion
  10.8 0.2 gather.15
  11.0 8.6 %scatter_custom_fusion.1 = bf16[480]{0:T(512)(128)(2,1)S(1)} fusion(s32[768]{0:T(1024)S(1)} %get-tuple-element.11, bf16[768]{0:T(1024)(128)(2,1)S(1)} %broadcast.296, bf16[]{:T(256)} %constant.117.clone.1), kind=kCustom, calls=%fused_computation.89 | custom fusion | bytes 962 | tf_op jit(solution)/shard_map/scatter | solution.py:63
  19.7 0.9 broadcast_multiply_fusion
  20.7 16.7 %all-to-all-start = ((bf16[32,15,512]{2,1,0:T(8,128)(2,1)}), bf16[32,15,512]{2,1,0:T(8,128)(2,1)S(1)}, u32[]{:S(2)}, u32[]{:S(2)}) async-start(bf16[32,15,512]{2,1,0:T(8,128)(2,1)} %broadcast_multiply_fusion), calls=%async_computation | async-start | bytes 1048576 | tf_op jit(solution)/shard_map/all_to_all | solution.py:71
  37.4 2.1 gather_fusion.1
  39.6 0.1 reshape.269
  39.8 0.1 reshape.324
  40.0 3.4 scatter_custom_fusion.2
  43.4 0.9 multiply_convert_fusion
  44.4 7.8 %all-to-all-done = bf16[32,15,512]{2,1,0:T(8,128)(2,1)S(1)} async-done(((bf16[32,15,512]{2,1,0:T(8,128)(2,1)}), bf16[32,15,512]{2,1,0:T(8,128)(2,1)S(1)}, u32[]{:S(2)}, u32[]{:S(2)}) %all-to-all-start) | async-done | bytes 491552 | tf_op jit(solution)/shard_map/all_to_all | solution.py:71
  52.2 5.7 %all-to-all-start.1 = ((bf16[32,15,512]{2,1,0:T(8,128)(2,1)}), bf16[32,15,512]{2,1,0:T(8,128)(2,1)S(1)}, u32[]{:S(2)}, u32[]{:S(2)}) async-start(bf16[32,15,512]{2,1,0:T(8,128)(2,1)} %multiply_convert_fusion), calls=%async_computation.1 | async-start | bytes 1048576 | tf_op jit(solution)/shard_map/all_to_all | solution.py:74
  58.0 0.2 reshape.262
  58.1 0.4 convolution_bitcast_fusion.4
  58.5 0.4 convolution_bitcast_fusion.5
  58.9 13.8 %all-to-all-done.1 = bf16[32,15,512]{2,1,0:T(8,128)(2,1)S(1)} async-done(((bf16[32,15,512]{2,1,0:T(8,128)(2,1)}), bf16[32,15,512]{2,1,0:T(8,128)(2,1)S(1)}, u32[]{:S(2)}, u32[]{:S(2)}) %all-to-all-start.1) | async-done | bytes 491552 | tf_op jit(solution)/shard_map/all_to_all | solution.py:74
  72.7 0.2 reshape.264
  72.8 1.5 convolution_bitcast_fusion.3
  74.4 0.2 pad_maximum_fusion
  74.6 2.1 collective-permute-start
  76.7 90.3 %collective-permute-done = f32[3,480,352]{1,2,0:T(8,128)S(1)} collective-permute-done((f32[3,480,352]{1,2,0:T(8,128)S(1)}, f32[3,480,352]{1,2,0:T(8,128)S(1)}, u32[]{:S(2)}, u32[]{:S(2)}) %collective-permute-start) | collective-permute-done | bytes 2027552 | tf_op jit(solution)/shard_map/ppermute | solution.py:18
  167.0 0.5 fusion.32
  167.5 6.7 %collective-permute-start.1 = (f32[3,480,352]{1,2,0:T(8,128)S(1)}, f32[3,480,352]{1,2,0:T(8,128)S(1)}, u32[]{:S(2)}, u32[]{:S(2)}) collective-permute-start(f32[3,480,352]{1,2,0:T(8,128)S(1)} %fusion.32), channel_id=1, source_target_pairs={{0,16},{16,0},{1,17},{17,1},{2,18},{18,2},{3,19},{19,3},{4,20},{20... | collective-permute-start | bytes 6082568 | tf_op jit(solution)/shard_map/ppermute | solution.py:18
  174.2 94.9 %collective-permute-done.1 = f32[3,480,352]{1,2,0:T(8,128)S(1)} collective-permute-done((f32[3,480,352]{1,2,0:T(8,128)S(1)}, f32[3,480,352]{1,2,0:T(8,128)S(1)}, u32[]{:S(2)}, u32[]{:S(2)}) %collective-permute-start.1) | collective-permute-done | bytes 2027552 | tf_op jit(solution)/shard_map/ppermute | solution.py:18
  269.1 0.8 fusion.40
  269.9 0.5 multiply_convert_fusion.3
  270.4 0.7 copy-done.6
  271.1 0.5 fusion.4
  271.6 0.5 fusion
  272.1 1.0 reshape.267
  273.0 6.6 %all-to-all-start.3 = ((bf16[32,15,512]{2,1,0:T(8,128)(2,1)}), bf16[32,15,512]{2,1,0:T(8,128)(2,1)S(1)}, u32[]{:S(2)}, u32[]{:S(2)}) async-start(bf16[32,15,512]{2,1,0:T(8,128)(2,1)} %reshape.267), calls=%async_computation.3 | async-start | bytes 1048576 | tf_op jit(solution)/shard_map/all_to_all | solution.py:107
  279.7 0.4 convolution_convert_fusion
  280.1 1.0 reshape.265
  281.1 13.3 %all-to-all-done.3 = bf16[32,15,512]{2,1,0:T(8,128)(2,1)S(1)} async-done(((bf16[32,15,512]{2,1,0:T(8,128)(2,1)}), bf16[32,15,512]{2,1,0:T(8,128)(2,1)S(1)}, u32[]{:S(2)}, u32[]{:S(2)}) %all-to-all-start.3) | async-done | bytes 491552 | tf_op jit(solution)/shard_map/all_to_all | solution.py:107
  294.4 5.9 %all-to-all-start.2 = ((bf16[32,15,512]{2,1,0:T(8,128)(2,1)}), bf16[32,15,512]{2,1,0:T(8,128)(2,1)}, u32[]{:S(2)}, u32[]{:S(2)}) async-start(bf16[32,15,512]{2,1,0:T(8,128)(2,1)} %reshape.265), calls=%async_computation.2 | async-start | bytes 1048576 | tf_op jit(solution)/shard_map/all_to_all | solution.py:106
  300.4 0.7 copy.26
  301.2 0.2 reshape.268
  301.4 3.3 gather_fusion.3
  304.7 1.3 reshape.271
  305.9 9.1 %all-to-all-done.2 = bf16[32,15,512]{2,1,0:T(8,128)(2,1)} async-done(((bf16[32,15,512]{2,1,0:T(8,128)(2,1)}), bf16[32,15,512]{2,1,0:T(8,128)(2,1)}, u32[]{:S(2)}, u32[]{:S(2)}) %all-to-all-start.2) | async-done | bytes 491552 | tf_op jit(solution)/shard_map/all_to_all | solution.py:106
  315.0 1.2 reshape.266
  316.3 3.3 gather_fusion.2
  319.6 2.5 reshape.270
  322.1 0.7 multiply_reduce_fusion
  322.8 0.9 copy-done.1
  323.7 0.7 multiply_reduce_fusion.1
  324.4 2.1 collective-permute-start.2
  326.6 1.2 convolution_bitcast_fusion.1
  327.8 6.6 %collective-permute-done.2 = f32[2,128,256]{2,1,0:T(8,128)S(1)} collective-permute-done((f32[2,128,256]{2,1,0:T(8,128)S(1)}, f32[2,128,256]{2,1,0:T(8,128)S(1)}, u32[]{:S(2)}, u32[]{:S(2)}) %collective-permute-start.2) | collective-permute-done | bytes 262176 | tf_op jit(solution)/shard_map/ppermute | solution.py:18
  334.4 15.7 %collective-permute-start.3 = (f32[2,128,128]{2,1,0:T(8,128)S(1)}, f32[2,128,128]{2,1,0:T(8,128)S(1)}, u32[]{:S(2)}, u32[]{:S(2)}) collective-permute-start(f32[2,128,128]{2,1,0:T(8,128)S(1)} %slice_select_fusion.1), channel_id=1, source_target_pairs={{0,2},{2,0},{1,3},{3,1},{4,6},{6,4},{5,7},{7,5},{8,10},{10,8},{9,1... | collective-permute-start | bytes 393224 | tf_op jit(solution)/shard_map/ppermute | solution.py:18
  350.1 1.2 convolution_bitcast_fusion.2
  351.3 2.0 collective-permute-done.3
  353.5 11.6 %collective-permute-start.4 = (f32[2,128,64]{2,1,0:T(8,128)S(1)}, f32[2,128,64]{2,1,0:T(8,128)S(1)}, u32[]{:S(2)}, u32[]{:S(2)}) collective-permute-start(f32[2,128,64]{2,1,0:T(8,128)S(1)} %slice_select_fusion), channel_id=1, source_target_pairs={{0,1},{1,0},{2,3},{3,2},{4,5},{5,4},{6,7},{7,6},{8,9},{9,8},{10,11... | collective-permute-start | bytes 196616 | tf_op jit(solution)/shard_map/ppermute | solution.py:18
  365.1 1.2 convolution_bitcast_fusion
  366.3 8.5 %collective-permute-done.4 = f32[2,128,64]{2,1,0:T(8,128)S(1)} collective-permute-done((f32[2,128,64]{2,1,0:T(8,128)S(1)}, f32[2,128,64]{2,1,0:T(8,128)S(1)}, u32[]{:S(2)}, u32[]{:S(2)}) %collective-permute-start.4) | collective-permute-done | bytes 65568 | tf_op jit(solution)/shard_map/ppermute | solution.py:18
  374.9 0.7 copy.28
  375.6 0.7 copy.29
  (53 shorter events, 1.2 us)
Async XLA Ops:
  0.6 57.9 %copy-start = (bf16[1,512,352]{1,2,0:T(8,128)(2,1)S(1)}, bf16[1,512,352]{1,2,0:T(8,128)(2,1)}, u32[]{:S(2)}) copy-start(bf16[1,512,352]{1,2,0:T(8,128)(2,1)} %param.11) | copy-start | bytes 1081348
  20.7 31.5 %all-to-all-start = ((bf16[32,15,512]{2,1,0:T(8,128)(2,1)}), bf16[32,15,512]{2,1,0:T(8,128)(2,1)S(1)}, u32[]{:S(2)}, u32[]{:S(2)}) async-start(bf16[32,15,512]{2,1,0:T(8,128)(2,1)} %broadcast_multiply_fusion), calls=%async_computation | async-start | bytes 1048576 | tf_op jit(solution)/shard_map/all_to_all | solution.py:71
  37.4 2.3 copy-start.15
  39.7 18.4 %copy-start.11 = (bf16[1,512,352]{1,2,0:T(8,128)(2,1)S(1)}, bf16[1,512,352]{1,2,0:T(8,128)(2,1)}, u32[]{:S(2)}) copy-start(bf16[1,512,352]{1,2,0:T(8,128)(2,1)} %param.12) | copy-start | bytes 1081348
  52.2 20.5 %all-to-all-start.1 = ((bf16[32,15,512]{2,1,0:T(8,128)(2,1)}), bf16[32,15,512]{2,1,0:T(8,128)(2,1)S(1)}, u32[]{:S(2)}, u32[]{:S(2)}) async-start(bf16[32,15,512]{2,1,0:T(8,128)(2,1)} %multiply_convert_fusion), calls=%async_computation.1 | async-start | bytes 1048576 | tf_op jit(solution)/shard_map/all_to_all | solution.py:74
  72.8 1.8 copy-start.2
  74.6 92.4 %collective-permute-start = (f32[3,480,352]{1,2,0:T(8,128)S(1)}, f32[3,480,352]{1,2,0:T(8,128)S(1)}, u32[]{:S(2)}, u32[]{:S(2)}) collective-permute-start(f32[3,480,352]{1,2,0:T(8,128)S(1)} %pad_maximum_fusion), channel_id=1, source_target_pairs={{0,8},{8,0},{1,9},{9,1},{2,10},{10,2},{3,11},{11,3},{4,12},{12,4},... | collective-permute-start | bytes 6082568 | tf_op jit(solution)/shard_map/ppermute | solution.py:18
  167.5 101.7 %collective-permute-start.1 = (f32[3,480,352]{1,2,0:T(8,128)S(1)}, f32[3,480,352]{1,2,0:T(8,128)S(1)}, u32[]{:S(2)}, u32[]{:S(2)}) collective-permute-start(f32[3,480,352]{1,2,0:T(8,128)S(1)} %fusion.32), channel_id=1, source_target_pairs={{0,16},{16,0},{1,17},{17,1},{2,18},{18,2},{3,19},{19,3},{4,20},{20... | collective-permute-start | bytes 6082568 | tf_op jit(solution)/shard_map/ppermute | solution.py:18
  269.9 1.7 copy-start.12
  270.4 0.7 copy-start.6
  270.4 1.2 copy-start.8
  270.4 9.3 %copy-start.4 = (bf16[1,480,352]{1,2,0:T(8,128)(2,1)}, bf16[1,480,352]{1,2,0:T(8,128)(2,1)S(1)}, u32[]{:S(2)}) copy-start(bf16[1,480,352]{1,2,0:T(8,128)(2,1)S(1)} %get-tuple-element.14) | copy-start | bytes 1013764
  271.6 8.1 %copy-start.10 = (bf16[1,512,352]{1,2,0:T(8,128)(2,1)S(1)}, bf16[1,512,352]{1,2,0:T(8,128)(2,1)}, u32[]{:S(2)}) copy-start(bf16[1,512,352]{1,2,0:T(8,128)(2,1)} %param.13) | copy-start | bytes 1081348
  273.0 27.3 %copy-start.14 = (s32[128,6]{0,1:T(8,128)S(1)}, s32[128,6]{0,1:T(8,128)}, u32[]{:S(2)}) copy-start(s32[128,6]{0,1:T(8,128)} %param.9) | copy-start | bytes 9220
  273.0 21.3 %all-to-all-start.3 = ((bf16[32,15,512]{2,1,0:T(8,128)(2,1)}), bf16[32,15,512]{2,1,0:T(8,128)(2,1)S(1)}, u32[]{:S(2)}, u32[]{:S(2)}) async-start(bf16[32,15,512]{2,1,0:T(8,128)(2,1)} %reshape.267), calls=%async_computation.3 | async-start | bytes 1048576 | tf_op jit(solution)/shard_map/all_to_all | solution.py:107
  294.4 20.7 %all-to-all-start.2 = ((bf16[32,15,512]{2,1,0:T(8,128)(2,1)}), bf16[32,15,512]{2,1,0:T(8,128)(2,1)}, u32[]{:S(2)}, u32[]{:S(2)}) async-start(bf16[32,15,512]{2,1,0:T(8,128)(2,1)} %reshape.265), calls=%async_computation.2 | async-start | bytes 1048576 | tf_op jit(solution)/shard_map/all_to_all | solution.py:106
  319.6 3.2 copy-start.13
  322.1 1.6 copy-start.1
  323.7 2.9 copy-start.9
  324.4 25.7 %copy-start.7 = (bf16[1,480,352]{1,2,0:T(8,128)(2,1)S(1)}, bf16[1,480,352]{1,2,0:T(8,128)(2,1)}, u32[]{:S(2)}) copy-start(bf16[1,480,352]{1,2,0:T(8,128)(2,1)} %copy-done.6) | copy-start | bytes 1013764
  324.4 9.9 %collective-permute-start.2 = (f32[2,128,256]{2,1,0:T(8,128)S(1)}, f32[2,128,256]{2,1,0:T(8,128)S(1)}, u32[]{:S(2)}, u32[]{:S(2)}) collective-permute-start(f32[2,128,256]{2,1,0:T(8,128)S(1)} %broadcast_select_fusion), channel_id=1, source_target_pairs={{0,4},{4,0},{1,5},{5,1},{2,6},{6,2},{3,7},{7,3},{8,12},{12,8},{9,1... | collective-permute-start | bytes 786440 | tf_op jit(solution)/shard_map/ppermute | solution.py:18
  327.8 37.3 %copy-start.3 = (bf16[480,512]{1,0:T(8,128)(2,1)S(1)}, bf16[480,512]{1,0:T(8,128)(2,1)}, u32[]{:S(2)}) copy-start(bf16[480,512]{1,0:T(8,128)(2,1)} %copy-done.2) | copy-start | bytes 1474564
  327.8 37.3 %copy-start.5 = (bf16[1,480,352]{1,2,0:T(8,128)(2,1)S(1)}, bf16[1,480,352]{1,2,0:T(8,128)(2,1)}, u32[]{:S(2)}) copy-start(bf16[1,480,352]{1,2,0:T(8,128)(2,1)} %copy-done.4) | copy-start | bytes 1013764
  334.4 19.0 %collective-permute-start.3 = (f32[2,128,128]{2,1,0:T(8,128)S(1)}, f32[2,128,128]{2,1,0:T(8,128)S(1)}, u32[]{:S(2)}, u32[]{:S(2)}) collective-permute-start(f32[2,128,128]{2,1,0:T(8,128)S(1)} %slice_select_fusion.1), channel_id=1, source_target_pairs={{0,2},{2,0},{1,3},{3,1},{4,6},{6,4},{5,7},{7,5},{8,10},{10,8},{9,1... | collective-permute-start | bytes 393224 | tf_op jit(solution)/shard_map/ppermute | solution.py:18
  353.5 21.3 %collective-permute-start.4 = (f32[2,128,64]{2,1,0:T(8,128)S(1)}, f32[2,128,64]{2,1,0:T(8,128)S(1)}, u32[]{:S(2)}, u32[]{:S(2)}) collective-permute-start(f32[2,128,64]{2,1,0:T(8,128)S(1)} %slice_select_fusion), channel_id=1, source_target_pairs={{0,1},{1,0},{2,3},{3,2},{4,5},{5,4},{6,7},{7,6},{8,9},{9,8},{10,11... | collective-permute-start | bytes 196616 | tf_op jit(solution)/shard_map/ppermute | solution.py:18
where the time goes:
time: 377 us; the launch traced here: 376 us
  waiting for transfers between devices  246 us (65%)
  starting transfers between devices  73.2 us (19%)
  local copies, waits for them, and re-layouts  40.8 us (11%)
  other arithmetic  7.6 us (2%)
  matrix products  7.25 us (2%)
    ppermute x5, waiting for transfers between devices, partner(): return lax.ppermute(block, axis, route)  202 us
    ppermute x5, starting transfers between devices, partner(): return lax.ppermute(block, axis, route)  38.2 us
    all_to_all x1, starting transfers between devices, on_device(): lax.all_to_all(sent_inputs.reshape(shape_out), 'own', split_axis=0, conca...  16.7 us
    all_to_all x1, waiting for transfers between devices, on_device(): lax.all_to_all(sent_cots.reshape(shape_out), 'own', split_axis=0, concat_...  13.8 us
    all_to_all x1, waiting for transfers between devices, on_device(): lax.all_to_all(grad_part.reshape(shape_out), 'own', split_axis=0, concat_...  13.3 us
    all_to_all x1, waiting for transfers between devices, on_device(): lax.all_to_all(out_part.reshape(shape_out), 'own', split_axis=0, concat_a...  9.1 us
    scatter x1, local copies, waits for them, and re-layouts, on_device(): row_used = jnp.zeros((row_total,), jnp.bfloat16).at[target].set(jnp.ones(...  8.61 us
    all_to_all x1, waiting for transfers between devices, on_device(): lax.all_to_all(sent_inputs.reshape(shape_out), 'own', split_axis=0, conca...  7.82 us
  transfers between devices with their start and end apart: 9, of which 9 were waited for; matrix products, arithmetic and copies ran while one was open for 5% of the time, Pallas kernels for 0%

commit v1 on v0

v1 whole, which is shorter than its diff:
```python
import jax
import jax.numpy as jnp
from jax import lax
from jax.experimental import pallas as pl
from jax.experimental.pallas import tpu as pltpu
from jax.sharding import PartitionSpec as P

OWN = 32
SLOT = 16
TOK = 128
DQ = 512
FQ = 352
TOP = 6
ROWS = OWN * SLOT
BPC = 8
CHUNK = BPC * SLOT
HALF = FQ // 2
MESH = pl.DeviceIdType.MESH
F32 = jnp.float32
BF16 = jnp.bfloat16


def mm(lhs, rhs, contract=(1, 0)):
    return lax.dot_general(
        lhs,
        rhs,
        (((contract[0],), (contract[1],)), ((), ())),
        preferred_element_type=F32,
    )


def iota(shape, dim):
    return lax.broadcasted_iota(jnp.int32, shape, dim)


def kernel(
    ids_ref,
    wts_ref,
    tok_hbm,
    cot_hbm,
    gate_hbm,
    up_hbm,
    down_hbm,
    layer_ref,
    tgrad_ref,
    gate_out,
    up_out,
    down_out,
    tok,
    cot,
    wgt,
    sel_t,
    whi_t,
    wlo_t,
    send,
    recv,
    far,
    relay,
    near,
    landed,
    hid,
    back,
    home,
    part,
    cx_out,
    cx_in,
    pieces,
    bx_out,
    bx_in,
    grads,
    in_sem,
    d_send,
    d_recv,
    far_send,
    far_recv,
    rs_send,
    rs_recv,
    ag_send,
    ag_recv,
    r_send,
    r_recv,
    cx_sem,
    bx_send,
    bx_recv,
    out_sem,
):
    me = lax.axis_index("own")
    grp = lax.axis_index("grp")
    zl, xx, core = me // 8, me % 8 // 2, me % 2
    yy, bb = grp // 4, grp % 4
    aa, cc = yy // 2, yy % 2
    zz = bb * 4 + zl
    above, below, across = (aa + 1) % 4, (aa + 3) % 4, (aa + 2) % 4
    dev_above = (me, (above * 2 + cc) * 4 + bb)
    dev_below = (me, (below * 2 + cc) * 4 + bb)
    dev_pair = (me, (aa * 2 + 1 - cc) * 4 + bb)

    def dev_own(other):
        zl2, core2 = other // 8, other % 2
        gap = (zl2 - zl + 4) % 4
        two = 2 - 4 * ((zl // 2 + core + core2) % 2)
        hop = jnp.where(gap == 2, two, jnp.where(gap == 3, -1, gap))
        return (other, yy * 4 + (zz + hop + 16) % 16 // 4)

    def dev_b(k):
        return (me, yy * 4 + (bb + k) % 4)

    def remote(src, dst, ssem, rsem, dev):
        return pltpu.make_async_remote_copy(
            src_ref=src,
            dst_ref=dst,
            send_sem=ssem,
            recv_sem=rsem,
            device_id=dev,
            device_id_type=MESH,
        )

    cols = pl.ds(pl.multiple_of(aa * DQ, DQ), DQ)
    loads = [
        pltpu.make_async_copy(tok_hbm.at[:, cols], tok, in_sem.at[0]),
        pltpu.make_async_copy(cot_hbm.at[:, cols], cot, in_sem.at[1]),
        pltpu.make_async_copy(gate_hbm, wgt.at[0], in_sem.at[2]),
        pltpu.make_async_copy(up_hbm, wgt.at[1], in_sem.at[3]),
        pltpu.make_async_copy(down_hbm, wgt.at[2], in_sem.at[4]),
    ]
    for load in loads:
        load.start()

    barrier = pltpu.get_barrier_semaphore()

    def greet(dev):
        pl.semaphore_signal(barrier, inc=1, device_id=dev, device_id_type=MESH)

    @pl.loop(1, OWN)
    def _(step):
        greet(dev_own((me + step) % OWN))

    for dev in (dev_above, dev_below, dev_pair, dev_b(1), dev_b(2), dev_b(3)):
        greet(dev)

    expert = iota((OWN, TOK), 0) * 2 + cc
    named = jnp.zeros((OWN, TOK), F32)
    weight = jnp.zeros((OWN, TOK), F32)
    for k in range(TOP):
        hit = ids_ref[k : k + 1, :] == expert
        named = jnp.where(hit, 1.0, named)
        weight = jnp.where(hit, wts_ref[k : k + 1, :], weight)
    earlier = (iota((TOK, TOK), 0) < iota((TOK, TOK), 1)).astype(F32).astype(BF16)
    place = mm(named.astype(BF16), earlier)
    place = jnp.where(named > 0.5, place, -1.0).astype(BF16)
    spread = (iota((ROWS, OWN), 0) // SLOT == iota((ROWS, OWN), 1)).astype(F32).astype(BF16)
    place_rows = mm(spread, place)
    taken = place_rows == (iota((ROWS, TOK), 0) % SLOT).astype(F32)
    w1 = weight.astype(BF16)
    rest = weight - w1.astype(F32)
    w2 = rest.astype(BF16)
    w3 = (rest - w2.astype(F32)).astype(BF16)
    weight_rows = mm(spread, w1) + mm(spread, w2) + mm(spread, w3)
    sel = jnp.where(taken, 1.0, 0.0)
    wsel = jnp.where(taken, weight_rows, 0.0)
    row_weight = jnp.sum(wsel, axis=1, keepdims=True)
    sel16 = sel.astype(BF16)

    loads[0].wait()
    send[0] = mm(sel16, tok[...]).astype(BF16).reshape(OWN, SLOT, DQ)
    loads[1].wait()
    send[1] = (row_weight * mm(sel16, cot[...])).astype(BF16).reshape(OWN, SLOT, DQ)

    pl.semaphore_wait(barrier, OWN - 1 + 6)

    for chunk in (across, above, below, aa):

        @pl.loop(0, BPC)
        def _(step, chunk=chunk):
            dl, core2 = step // 2, step % 2
            other = (zl - dl + 4) % 4 * 8 + (xx + dl - chunk + 8) % 4 * 2 + core2
            pos = chunk * BPC + dl * 2 + core

            @pl.when(other == me)
            def _():
                pltpu.make_async_copy(send.at[:, other], recv.at[:, pos], d_recv.at[chunk]).start()

            @pl.when(other != me)
            def _():
                remote(
                    send.at[:, other], recv.at[:, pos], d_send, d_recv.at[chunk], dev_own(other)
                ).start()

    wsel_t = wsel.T
    hi = wsel_t.astype(BF16)
    whi_t[...] = hi
    wlo_t[...] = (wsel_t - hi.astype(F32)).astype(BF16)
    sel_t[...] = sel.T.astype(BF16)
    for load in loads[2:]:
        load.wait()

    lower, upper = pl.ds(0, HALF), pl.ds(HALF, HALF)

    def rows_of(chunk):
        return pl.ds(chunk * BPC, BPC)

    def lanes_of(chunk):
        return pl.ds(pl.multiple_of(chunk * CHUNK, CHUNK), CHUNK)

    def partials(chunk):
        block = recv.at[:, rows_of(chunk)]
        pltpu.make_async_copy(block, block, d_recv.at[chunk]).wait()
        x_rows = recv[0, rows_of(chunk)].reshape(CHUNK, DQ)
        c_rows = recv[1, rows_of(chunk)].reshape(CHUNK, DQ)
        return [mm(wgt[t], rows, (1, 1)) for t, rows in enumerate((x_rows, x_rows, c_rows))]

    for t, value in enumerate(partials(across)):
        far[t] = value.astype(BF16)
    far_copies = [
        remote(far.at[:, lower], relay.at[0], far_send.at[0], far_recv.at[0], dev_above),
        remote(far.at[:, upper], relay.at[1], far_send.at[1], far_recv.at[1], dev_below),
    ]
    for copy in far_copies:
        copy.start()
    rs_copies = []
    for way, chunk, dev in ((0, above, dev_above), (1, below, dev_below)):
        values = partials(chunk)
        far_copies[way].wait_recv()
        for t, value in enumerate(values):
            first, second = value[:HALF], value[HALF:]
            if way == 0:
                first = first + relay[0, t].astype(F32)
            else:
                second = second + relay[1, t].astype(F32)
            near[way, t, :HALF] = first.astype(BF16)
            near[way, t, HALF:] = second.astype(BF16)
        copy = remote(near.at[way], landed.at[way], rs_send.at[way], rs_recv.at[way], dev)
        copy.start()
        rs_copies.append(copy)
    mine = partials(aa)
    for copy in rs_copies:
        copy.wait_recv()
    gating, up_proj, grad_hidden = [
        value + landed[0, t].astype(F32) + landed[1, t].astype(F32) for t, value in enumerate(mine)
    ]
    sigma = jax.nn.sigmoid(gating)
    grad_gate = grad_hidden * up_proj * sigma * (1.0 + gating * (1.0 - sigma))
    hid[0, :, lanes_of(aa)] = (gating * sigma * up_proj).astype(BF16)
    hid[1, :, lanes_of(aa)] = grad_gate.astype(BF16)
    hid[2, :, lanes_of(aa)] = (grad_hidden * gating * sigma).astype(BF16)

    def pass_on(index, chunk, half, dev):
        block = hid.at[:, half, lanes_of(chunk)]
        return remote(block, block, ag_send.at[index], ag_recv.at[index], dev)

    up_a = pass_on(0, aa, lower, dev_above)
    down_b = pass_on(1, aa, upper, dev_below)
    up_b = pass_on(2, aa, upper, dev_above)
    down_a = pass_on(3, aa, lower, dev_below)
    for copy in (up_a, down_b, up_b, down_a):
        copy.start()

    def arrived(index, chunk, half):
        block = hid.at[:, half, lanes_of(chunk)]
        pltpu.make_async_copy(block, block, ag_recv.at[index]).wait()

    def give_back(chunk):
        lanes = lanes_of(chunk)
        out_rows = mm(hid[0, :, lanes], wgt[2], (0, 0))
        grad_rows = mm(hid[1, :, lanes], wgt[0], (0, 0)) + mm(hid[2, :, lanes], wgt[1], (0, 0))
        back[0, rows_of(chunk)] = out_rows.astype(BF16).reshape(BPC, SLOT, DQ)
        back[1, rows_of(chunk)] = grad_rows.astype(BF16).reshape(BPC, SLOT, DQ)

        @pl.loop(0, BPC)
        def _(step):
            dl, core2 = step // 2, step % 2
            other = (zl + dl) % 4 * 8 + (xx + chunk - dl + 4) % 4 * 2 + core2
            pos = chunk * BPC + step

            @pl.when(other == me)
            def _():
                pltpu.make_async_copy(back.at[:, pos], home.at[:, me], r_recv).start()

            @pl.when(other != me)
            def _():
                remote(back.at[:, pos], home.at[:, me], r_send, r_recv, dev_own(other)).start()

    give_back(aa)
    arrived(0, below, lower)
    on_up = pass_on(4, below, lower, dev_above)
    on_up.start()
    arrived(1, above, upper)
    on_down = pass_on(5, above, upper, dev_below)
    on_down.start()
    arrived(2, below, upper)
    give_back(below)
    arrived(3, above, lower)
    give_back(above)
    arrived(4, across, lower)
    arrived(5, across, upper)
    give_back(across)

    stores = []
    for t, (side, kind, out) in enumerate(((0, 1, gate_out), (0, 2, up_out), (1, 0, down_out))):
        grads[t] = mm(hid[kind], recv[side].reshape(ROWS, DQ))
        store = pltpu.make_async_copy(grads.at[t], out, out_sem.at[t])
        store.start()
        stores.append(store)

    pltpu.make_async_copy(home, home, r_recv).wait()
    out_home = home[0].reshape(ROWS, DQ)
    part[0] = mm(whi_t[...], out_home) + mm(wlo_t[...], out_home)
    part[1] = mm(sel_t[...], home[1].reshape(ROWS, DQ))

    kept = pl.ds(pl.multiple_of(cc * 256, 256), 256)
    given = pl.ds(pl.multiple_of((1 - cc) * 256, 256), 256)
    cx_out[...] = part[:, :, given].astype(BF16)
    cx = remote(cx_out, cx_in, cx_sem.at[0], cx_sem.at[1], dev_pair)
    cx.start()
    cx.wait_recv()
    total = part[:, :, kept] + cx_in[...].astype(F32)
    for p in range(4):
        piece = jnp.concatenate(
            [total[0, :, 64 * p : 64 * p + 64], total[1, :, 64 * p : 64 * p + 64]], axis=1
        )
        pieces[p] = piece
        bx_out[p] = piece.astype(BF16)
    bx = []
    for k in (1, 2, 3):
        copy = remote(
            bx_out.at[(bb + k) % 4],
            bx_in.at[k - 1],
            bx_send.at[k - 1],
            bx_recv.at[k - 1],
            dev_b(k),
        )
        copy.start()
        bx.append(copy)
    final = pieces[bb]
    for k in range(3):
        bx[k].wait_recv()
        final = final + bx_in[k].astype(F32)
    layer_ref[...] = final[:, :64].astype(BF16)
    tgrad_ref[...] = final[:, 64:].astype(BF16)

    pltpu.make_async_copy(send.at[:, : OWN - 1], recv.at[:, : OWN - 1], d_send).wait()
    pltpu.make_async_copy(back.at[:, : OWN - 1], home.at[:, : OWN - 1], r_send).wait()
    for copy in far_copies + rs_copies + [up_a, down_b, up_b, down_a, on_up, on_down, cx] + bx:
        copy.wait_send()
    for store in stores:
        store.wait()


def on_device(tokens, cotangent, route_ids, route_weights, gate_weight, up_weight, down_weight_t):
    vmem = pl.BlockSpec(memory_space=pltpu.VMEM)
    hbm = pl.BlockSpec(memory_space=pl.ANY)
    dma = pltpu.SemaphoreType.DMA
    grad_shape = jax.ShapeDtypeStruct((FQ, DQ), F32)
    out_shape = jax.ShapeDtypeStruct((TOK, 64), BF16)
    layer_out, token_grad, gate_grad, up_grad, down_grad = pl.pallas_call(
        kernel,
        out_shape=(out_shape, out_shape, grad_shape, grad_shape, grad_shape),
        in_specs=[vmem, vmem, hbm, hbm, hbm, hbm, hbm],
        out_specs=(vmem, vmem, hbm, hbm, hbm),
        scratch_shapes=[
            pltpu.VMEM((TOK, DQ), BF16),
            pltpu.VMEM((TOK, DQ), BF16),
            pltpu.VMEM((3, FQ, DQ), BF16),
            pltpu.VMEM((TOK, ROWS), BF16),
            pltpu.VMEM((TOK, ROWS), BF16),
            pltpu.VMEM((TOK, ROWS), BF16),
            pltpu.VMEM((2, OWN, SLOT, DQ), BF16),
            pltpu.VMEM((2, OWN, SLOT, DQ), BF16),
            pltpu.VMEM((3, FQ, CHUNK), BF16),
            pltpu.VMEM((2, 3, HALF, CHUNK), BF16),
            pltpu.VMEM((2, 3, FQ, CHUNK), BF16),
            pltpu.VMEM((2, 3, FQ, CHUNK), BF16),
            pltpu.VMEM((3, FQ, ROWS), BF16),
            pltpu.VMEM((2, OWN, SLOT, DQ), BF16),
            pltpu.VMEM((2, OWN, SLOT, DQ), BF16),
            pltpu.VMEM((2, TOK, DQ), F32),
            pltpu.VMEM((2, TOK, 256), BF16),
            pltpu.VMEM((2, TOK, 256), BF16),
            pltpu.VMEM((4, TOK, 128), F32),
            pltpu.VMEM((4, TOK, 128), BF16),
            pltpu.VMEM((3, TOK, 128), BF16),
            pltpu.VMEM((3, FQ, DQ), F32),
            dma((5,)),
            dma,
            dma((4,)),
            dma((2,)),
            dma((2,)),
            dma((2,)),
            dma((2,)),
            dma((6,)),
            dma((6,)),
            dma,
            dma,
            dma((2,)),
            dma((3,)),
            dma((3,)),
            dma((3,)),
        ],
        compiler_params=pltpu.CompilerParams(
            collective_id=0, has_side_effects=True, vmem_limit_bytes=40 * 1024 * 1024
        ),
        cost_estimate=pl.CostEstimate(
            flops=2 * 9 * ROWS * DQ * FQ, bytes_accessed=8 * 1024 * 1024, transcendentals=CHUNK * FQ
        ),
    )(
        route_ids.T,
        route_weights.T,
        tokens,
        cotangent,
        gate_weight[0].T,
        up_weight[0].T,
        down_weight_t[0].T,
    )
    return (layer_out, token_grad, gate_grad.T[None], up_grad.T[None], down_grad.T[None])


def solution(mesh):
    placed = (
        P("own", None),
        P("own", None),
        P("own", None),
        P("own", None),
        P(("own", "grp"), None, None),
        P(("own", "grp"), None, None),
        P(("own", "grp"), None, None),
    )
    return jax.shard_map(
        on_device,
        mesh=mesh,
        in_specs=placed,
        out_specs=(
            P("own", "grp"),
            P("own", "grp"),
            P(("own", "grp"), None, None),
            P(("own", "grp"), None, None),
            P(("own", "grp"), None, None),
        ),
        check_vma=False,
    )
```

time: 377 us -> 114 us (0.30)
  the two profiles are of different devices: /device:TPU:4 before, /device:TPU:7 now
where the time goes in v1:
time: 114 us
  Pallas kernels  103 us (90%)
  local copies, waits for them, and re-layouts  9.68 us (8%)
    pallas_call x1, Pallas kernels, on_device(): pl.pallas_call(kernel, out_shape=(out_shape, out_shape, grad_shape, grad_...  103 us
    unnamed x19, local copies, waits for them, and re-layouts  9.68 us

profile of v1, /device:TPU:7, one launch (start us, length us, event | category | flops | bytes accessed | tf_op | source)
XLA Modules:
  0.0 113.8 jit_solution(14750582394801835449)
XLA Ops:
  0.6 0.0 copy-start.6
  0.6 0.0 copy-start.5
  0.7 0.7 copy-done.6
  1.3 0.0 copy-done.5
  1.3 0.0 copy-start
  1.3 1.0 copy-done
  2.4 0.0 copy-start.1
  2.4 1.0 copy-done.1
  3.4 0.0 copy-start.2
  3.4 1.0 copy-done.2
  4.4 0.0 copy-start.3
  4.4 1.0 copy-done.3
  5.4 0.0 copy-start.4
  5.4 1.0 copy-done.4
  6.4 103.5 %shard_map.110 = (bf16[128,64]{1,0:T(8,128)(2,1)S(1)}, bf16[128,64]{1,0:T(8,128)(2,1)S(1)}, f32[352,512]{1,0:T(8,128)S(1)}, f32[352,512]{1,0:T(8,128)S(1)}, f32[352,512]{1,0:T(8,128)S(1)}) custom-call(s32[6,128]{1,0:T(8,128)S(1)} %bitcast.26, f32[6,128]{1,0:T(8,128)S(1)} %bitcast.27, bf16[128,2048]{1,0:T(8,128)(2,1)S(1)} %copy-done, ...), custom_call_target="tpu_custom_call" | custom-call | flops 1660944384 | bytes 8388608 | tf_op jit(solution)/shard_map/pallas_call | solution.py:355
  109.8 0.7 copy.12
  110.5 0.7 copy.13
  111.2 0.9 copy.17
  112.1 0.9 copy.18
  113.0 0.9 copy.19
Async XLA Ops:
  0.6 0.7 copy-start.6
  0.6 0.7 copy-start.5
  1.3 1.0 copy-start
  2.4 1.0 copy-start.1
  3.4 1.0 copy-start.2
  4.4 1.0 copy-start.3
  5.4 1.0 copy-start.4

commit v2 on v1

v2 whole, which is shorter than its diff:
```python
import jax
import jax.numpy as jnp
from jax import lax
from jax.experimental import pallas as pl
from jax.experimental.pallas import tpu as pltpu
from jax.sharding import PartitionSpec as P

OWN = 32
SLOT = 16
TOK = 128
DQ = 512
FQ = 352
TOP = 6
ROWS = OWN * SLOT
BPC = 8
CHUNK = BPC * SLOT
QUARTERS = ((0, 96), (96, 80), (176, 96), (272, 80))
UP, DOWN = 0, 1
RELAYED = ((0, 1), (2, 3))
VMEM_LIMIT = 58 * 1024 * 1024
MESH = pl.DeviceIdType.MESH
F32 = jnp.float32
BF16 = jnp.bfloat16


def mm(lhs, rhs, contract=(1, 0)):
    return lax.dot_general(
        lhs,
        rhs,
        (((contract[0],), (contract[1],)), ((), ())),
        preferred_element_type=F32,
    )


def iota(shape, dim):
    return lax.broadcasted_iota(jnp.int32, shape, dim)


def kernel(
    ids_hbm,
    wts_hbm,
    tok_hbm,
    cot_hbm,
    gate_hbm,
    up_hbm,
    down_hbm,
    layer_ref,
    tgrad_ref,
    gate_out,
    up_out,
    down_out,
    ids_ref,
    wts_ref,
    tok,
    cot,
    wgt,
    sel16,
    row_w,
    sel_t,
    whi_t,
    wlo_t,
    send,
    recv,
    far,
    relay,
    near,
    keep,
    mine,
    landed,
    hid,
    back,
    home,
    part,
    cx_out,
    cx_in,
    pieces,
    bx_out,
    bx_in,
    in_sem,
    d_send,
    d_recv,
    far_send,
    far_recv,
    rs_send,
    rs_recv,
    ag_send,
    ag_recv,
    fw_send,
    fw_recv,
    r_send,
    r_recv,
    cx_sem,
    bx_send,
    bx_recv,
):
    me = lax.axis_index("own")
    grp = lax.axis_index("grp")
    zl, xx, core = me // 8, me % 8 // 2, me % 2
    yy, bb = grp // 4, grp % 4
    aa, cc = yy // 2, yy % 2
    zz = bb * 4 + zl
    above, below, across = (aa + 1) % 4, (aa + 3) % 4, (aa + 2) % 4
    dev_above = (me, (above * 2 + cc) * 4 + bb)
    dev_below = (me, (below * 2 + cc) * 4 + bb)
    dev_pair = (me, (aa * 2 + 1 - cc) * 4 + bb)

    def dev_own(other):
        zl2, core2 = other // 8, other % 2
        gap = (zl2 - zl + 4) % 4
        two = 2 - 4 * ((zl // 2 + core + core2) % 2)
        hop = jnp.where(gap == 2, two, jnp.where(gap == 3, -1, gap))
        return (other, yy * 4 + (zz + hop + 16) % 16 // 4)

    def dev_b(k):
        return (me, yy * 4 + (bb + k) % 4)

    def remote(src, dst, ssem, rsem, dev):
        return pltpu.make_async_remote_copy(
            src_ref=src,
            dst_ref=dst,
            send_sem=ssem,
            recv_sem=rsem,
            device_id=dev,
            device_id_type=MESH,
        )

    cols = pl.ds(pl.multiple_of(aa * DQ, DQ), DQ)
    loads = [
        pltpu.make_async_copy(ids_hbm, ids_ref, in_sem.at[5]),
        pltpu.make_async_copy(wts_hbm, wts_ref, in_sem.at[6]),
        pltpu.make_async_copy(tok_hbm.at[:, cols], tok, in_sem.at[0]),
        pltpu.make_async_copy(cot_hbm.at[:, cols], cot, in_sem.at[1]),
        pltpu.make_async_copy(gate_hbm, wgt.at[0], in_sem.at[2]),
        pltpu.make_async_copy(up_hbm, wgt.at[1], in_sem.at[3]),
        pltpu.make_async_copy(down_hbm, wgt.at[2], in_sem.at[4]),
    ]
    for load in loads:
        load.start()

    barrier = pltpu.get_barrier_semaphore()

    def greet(dev):
        pl.semaphore_signal(barrier, inc=1, device_id=dev, device_id_type=MESH)

    @pl.loop(1, OWN)
    def _(step):
        greet(dev_own((me + step) % OWN))

    for dev in (dev_above, dev_below, dev_pair, dev_b(1), dev_b(2), dev_b(3)):
        greet(dev)

    loads[0].wait()
    loads[1].wait()
    expert = iota((OWN, TOK), 0) * 2 + cc
    named = jnp.zeros((OWN, TOK), F32)
    weight = jnp.zeros((OWN, TOK), F32)
    for k in range(TOP):
        hit = ids_ref[k : k + 1, :] == expert
        named = jnp.where(hit, 1.0, named)
        weight = jnp.where(hit, wts_ref[k : k + 1, :], weight)
    earlier = (iota((TOK, TOK), 0) < iota((TOK, TOK), 1)).astype(F32).astype(BF16)
    place = mm(named.astype(BF16), earlier)
    place = jnp.where(named > 0.5, place, -1.0).astype(BF16)
    pos_of = iota((ROWS, OWN), 0) // SLOT
    step_of = pos_of % BPC // 2
    owner_of = (zl - step_of + 4) % 4 * 8 + (xx + step_of - pos_of // BPC + 8) % 4 * 2 + pos_of % 2
    spread = (owner_of == iota((ROWS, OWN), 1)).astype(F32).astype(BF16)
    place_rows = mm(spread, place)
    taken = place_rows == (iota((ROWS, TOK), 0) % SLOT).astype(F32)
    w1 = weight.astype(BF16)
    rest = weight - w1.astype(F32)
    w2 = rest.astype(BF16)
    w3 = (rest - w2.astype(F32)).astype(BF16)
    weight_rows = mm(spread, w1) + mm(spread, w2) + mm(spread, w3)
    sel = jnp.where(taken, 1.0, 0.0)
    wsel = jnp.where(taken, weight_rows, 0.0)
    row_weight = jnp.sum(wsel, axis=1, keepdims=True)
    sel16[...] = sel.astype(BF16)
    row_w[...] = row_weight

    for load in loads[2:4]:
        load.wait()

    def rows_of(chunk):
        return pl.ds(chunk * BPC, BPC)

    def lanes_of(chunk):
        return pl.ds(pl.multiple_of(chunk * CHUNK, CHUNK), CHUNK)

    for order, chunk in enumerate((across, above, below, aa)):
        picks = sel16[lanes_of(chunk), :]
        x_rows = mm(picks, tok[...])
        c_rows = row_w[lanes_of(chunk), :] * mm(picks, cot[...])
        send[0, rows_of(chunk)] = x_rows.astype(BF16).reshape(BPC, SLOT, DQ)
        send[1, rows_of(chunk)] = c_rows.astype(BF16).reshape(BPC, SLOT, DQ)
        if order == 0:
            pl.semaphore_wait(barrier, OWN - 1 + 6)

        @pl.loop(0, BPC)
        def _(step, chunk=chunk):
            dl, core2 = step // 2, step % 2
            other = (zl - dl + 4) % 4 * 8 + (xx + dl - chunk + 8) % 4 * 2 + core2
            src = send.at[:, chunk * BPC + step]
            dst = recv.at[:, chunk * BPC + dl * 2 + core]

            @pl.when(other == me)
            def _():
                pltpu.make_async_copy(src, dst, d_recv.at[chunk]).start()

            @pl.when(other != me)
            def _():
                remote(src, dst, d_send, d_recv.at[chunk], dev_own(other)).start()

    wsel_t = wsel.T
    hi = wsel_t.astype(BF16)
    whi_t[...] = hi
    wlo_t[...] = (wsel_t - hi.astype(F32)).astype(BF16)
    sel_t[...] = sel.T.astype(BF16)
    for load in loads[4:]:
        load.wait()

    def partials(chunk):
        block = recv.at[:, rows_of(chunk)]
        pltpu.make_async_copy(block, block, d_recv.at[chunk]).wait()
        x_rows = recv[0, rows_of(chunk)].reshape(CHUNK, DQ)
        c_rows = recv[1, rows_of(chunk)].reshape(CHUNK, DQ)
        return [mm(wgt[t], rows, (1, 1)) for t, rows in enumerate((x_rows, x_rows, c_rows))]

    def units(quarter):
        return pl.ds(*QUARTERS[quarter])

    devs = (dev_above, dev_below)
    copies = {}

    def go(kind, way, quarter, src, dst, sems):
        index = 4 * way + quarter
        copy = remote(src, dst, sems[0].at[index], sems[1].at[index], devs[way])
        copy.start()
        copies[kind, way, quarter] = copy

    def send_near(way, quarter):
        block = (way, slice(None), units(quarter))
        go("near", way, quarter, near.at[block], landed.at[block], (rs_send, rs_recv))

    for t, value in enumerate(partials(across)):
        far[t] = value.astype(BF16)
    for i in range(2):
        for way in (UP, DOWN):
            quarter = RELAYED[way][i]
            block = (slice(None), units(quarter))
            go("far", way, quarter, far.at[block], relay.at[block], (far_send, far_recv))
    for way, chunk in ((UP, above), (DOWN, below)):
        for t, value in enumerate(partials(chunk)):
            keep[way, t] = value
            near[way, t] = value.astype(BF16)
        send_near(way, RELAYED[1 - way][0])
    for i in range(2):
        for way in (UP, DOWN):
            quarter = RELAYED[way][i]
            copies["far", way, quarter].wait_recv()
            summed = keep[way, :, units(quarter)] + relay[:, units(quarter)].astype(F32)
            near[way, :, units(quarter)] = summed.astype(BF16)
            send_near(way, quarter)
        if i == 0:
            for way in (UP, DOWN):
                send_near(way, RELAYED[1 - way][1])
            for t, value in enumerate(partials(aa)):
                mine[t] = value

    def pass_on(kind, way, chunk, quarter, sems):
        block = hid.at[:, units(quarter), lanes_of(chunk)]
        go(kind, way, quarter, block, block, sems)

    def arrived(sems, way, chunk, quarter):
        block = hid.at[:, units(quarter), lanes_of(chunk)]
        pltpu.make_async_copy(block, block, sems.at[4 * way + quarter]).wait()

    for quarter in (0, 2, 1, 3):
        copies["near", UP, quarter].wait_recv()
        copies["near", DOWN, quarter].wait_recv()
        span = units(quarter)
        gating, up_proj, grad_hidden = [
            mine[t, span] + landed[UP, t, span].astype(F32) + landed[DOWN, t, span].astype(F32)
            for t in range(3)
        ]
        sigma = jax.nn.sigmoid(gating)
        grad_gate = grad_hidden * up_proj * sigma * (1.0 + gating * (1.0 - sigma))
        hid[0, span, lanes_of(aa)] = (gating * sigma * up_proj).astype(BF16)
        hid[1, span, lanes_of(aa)] = grad_gate.astype(BF16)
        hid[2, span, lanes_of(aa)] = (grad_hidden * gating * sigma).astype(BF16)
        first = UP if quarter in RELAYED[UP] else DOWN
        for way in (first, 1 - first):
            pass_on("own", way, aa, quarter, (ag_send, ag_recv))

    def give_back(chunk):
        lanes = lanes_of(chunk)
        out_rows = mm(hid[0, :, lanes], wgt[2], (0, 0))
        grad_rows = mm(hid[1, :, lanes], wgt[0], (0, 0)) + mm(hid[2, :, lanes], wgt[1], (0, 0))
        back[0, rows_of(chunk)] = out_rows.astype(BF16).reshape(BPC, SLOT, DQ)
        back[1, rows_of(chunk)] = grad_rows.astype(BF16).reshape(BPC, SLOT, DQ)

        @pl.loop(0, BPC)
        def _(step):
            dl, core2 = step // 2, step % 2
            other = (zl + dl) % 4 * 8 + (xx + chunk - dl + 4) % 4 * 2 + core2
            src = back.at[:, chunk * BPC + step]
            dst = home.at[:, chunk * BPC + dl * 2 + core]

            @pl.when(other == me)
            def _():
                pltpu.make_async_copy(src, dst, r_recv.at[chunk]).start()

            @pl.when(other != me)
            def _():
                remote(src, dst, r_send, r_recv.at[chunk], dev_own(other)).start()

    for i in range(2):
        for way, chunk in ((UP, below), (DOWN, above)):
            quarter = RELAYED[way][i]
            arrived(ag_recv, way, chunk, quarter)
            pass_on("on", way, chunk, quarter, (fw_send, fw_recv))
        if i == 0:
            give_back(aa)
    for way, chunk in ((UP, below), (DOWN, above)):
        for quarter in RELAYED[1 - way]:
            arrived(ag_recv, way, chunk, quarter)
        give_back(chunk)
    for way in (UP, DOWN):
        for quarter in RELAYED[way]:
            arrived(fw_recv, way, across, quarter)
    give_back(across)

    def combine(chunk):
        block = home.at[:, rows_of(chunk)]
        pltpu.make_async_copy(block, block, r_recv.at[chunk]).wait()
        lanes = lanes_of(chunk)
        out_home = home[0, rows_of(chunk)].reshape(CHUNK, DQ)
        grad_home = home[1, rows_of(chunk)].reshape(CHUNK, DQ)
        return (
            mm(whi_t[:, lanes], out_home) + mm(wlo_t[:, lanes], out_home),
            mm(sel_t[:, lanes], grad_home),
        )

    part[0], part[1] = combine(aa)
    for chunk in (below, above):
        layer, tgrad = combine(chunk)
        part[0] += layer
        part[1] += tgrad

    for side, kind, out in ((0, 1, gate_out), (0, 2, up_out), (1, 0, down_out)):
        out[...] = mm(hid[kind], recv[side].reshape(ROWS, DQ))

    layer, tgrad = combine(across)
    part[0] += layer
    part[1] += tgrad

    kept = pl.ds(pl.multiple_of(cc * 256, 256), 256)
    given = pl.ds(pl.multiple_of((1 - cc) * 256, 256), 256)
    cx_out[...] = part[:, :, given].astype(BF16)
    cx = remote(cx_out, cx_in, cx_sem.at[0], cx_sem.at[1], dev_pair)
    cx.start()
    cx.wait_recv()
    total = part[:, :, kept] + cx_in[...].astype(F32)
    for p in range(4):
        piece = jnp.concatenate(
            [total[0, :, 64 * p : 64 * p + 64], total[1, :, 64 * p : 64 * p + 64]], axis=1
        )
        pieces[p] = piece
        bx_out[p] = piece.astype(BF16)
    bx = []
    for k in (1, 2, 3):
        copy = remote(
            bx_out.at[(bb + k) % 4],
            bx_in.at[k - 1],
            bx_send.at[k - 1],
            bx_recv.at[k - 1],
            dev_b(k),
        )
        copy.start()
        bx.append(copy)
    final = pieces[bb]
    for k in range(3):
        bx[k].wait_recv()
        final = final + bx_in[k].astype(F32)
    final = final.T
    layer_ref[...] = final[:64].astype(BF16)
    tgrad_ref[...] = final[64:].astype(BF16)

    pltpu.make_async_copy(send.at[:, : OWN - 1], recv.at[:, : OWN - 1], d_send).wait()
    pltpu.make_async_copy(back.at[:, : OWN - 1], home.at[:, : OWN - 1], r_send).wait()
    for copy in list(copies.values()) + [cx] + bx:
        copy.wait_send()


def finish(*refs):
    given, out, held = refs[:5], refs[5:10], refs[10:15]
    in_sem, out_sem = refs[15:]
    loads = [pltpu.make_async_copy(given[i], held[i], in_sem.at[i]) for i in range(5)]
    stores = [pltpu.make_async_copy(held[i], out[i], out_sem.at[i]) for i in range(5)]
    for load in loads:
        load.start()
    for load, store in zip(loads, stores):
        load.wait()
        store.start()
    for store in stores:
        store.wait()


def on_device(tokens, cotangent, route_ids, route_weights, gate_weight, up_weight, down_weight_t):
    vmem = pl.BlockSpec(memory_space=pltpu.VMEM)
    hbm = pl.BlockSpec(memory_space=pl.ANY)
    dma = pltpu.SemaphoreType.DMA
    grad_shape = jax.ShapeDtypeStruct((FQ, DQ), F32)
    out_shape = jax.ShapeDtypeStruct((64, TOK), BF16)
    out_shapes = (out_shape, out_shape, grad_shape, grad_shape, grad_shape)
    results = pl.pallas_call(
        kernel,
        out_shape=out_shapes,
        in_specs=[hbm] * 7,
        out_specs=(vmem,) * 5,
        scratch_shapes=[
            pltpu.VMEM((TOP, TOK), jnp.int32),
            pltpu.VMEM((TOP, TOK), F32),
            pltpu.VMEM((TOK, DQ), BF16),
            pltpu.VMEM((TOK, DQ), BF16),
            pltpu.VMEM((3, FQ, DQ), BF16),
            pltpu.VMEM((ROWS, TOK), BF16),
            pltpu.VMEM((ROWS, 1), F32),
            pltpu.VMEM((TOK, ROWS), BF16),
            pltpu.VMEM((TOK, ROWS), BF16),
            pltpu.VMEM((TOK, ROWS), BF16),
            pltpu.VMEM((2, OWN, SLOT, DQ), BF16),
            pltpu.VMEM((2, OWN, SLOT, DQ), BF16),
            pltpu.VMEM((3, FQ, CHUNK), BF16),
            pltpu.VMEM((3, FQ, CHUNK), BF16),
            pltpu.VMEM((2, 3, FQ, CHUNK), BF16),
            pltpu.VMEM((2, 3, FQ, CHUNK), F32),
            pltpu.VMEM((3, FQ, CHUNK), F32),
            pltpu.VMEM((2, 3, FQ, CHUNK), BF16),
            pltpu.VMEM((3, FQ, ROWS), BF16),
            pltpu.VMEM((2, OWN, SLOT, DQ), BF16),
            pltpu.VMEM((2, OWN, SLOT, DQ), BF16),
            pltpu.VMEM((2, TOK, DQ), F32),
            pltpu.VMEM((2, TOK, 256), BF16),
            pltpu.VMEM((2, TOK, 256), BF16),
            pltpu.VMEM((4, TOK, 128), F32),
            pltpu.VMEM((4, TOK, 128), BF16),
            pltpu.VMEM((3, TOK, 128), BF16),
            dma((7,)),
            dma,
            dma((4,)),
            dma((8,)),
            dma((8,)),
            dma((8,)),
            dma((8,)),
            dma((8,)),
            dma((8,)),
            dma((8,)),
            dma((8,)),
            dma,
            dma((4,)),
            dma((2,)),
            dma((3,)),
            dma((3,)),
        ],
        compiler_params=pltpu.CompilerParams(
            collective_id=0, has_side_effects=True, vmem_limit_bytes=VMEM_LIMIT
        ),
        cost_estimate=pl.CostEstimate(
            flops=2 * 9 * ROWS * DQ * FQ, bytes_accessed=8 * 1024 * 1024, transcendentals=CHUNK * FQ
        ),
    )(
        route_ids.T,
        route_weights.T,
        tokens,
        cotangent,
        gate_weight[0].T,
        up_weight[0].T,
        down_weight_t[0].T,
    )
    layer_out, token_grad, gate_grad, up_grad, down_grad = pl.pallas_call(
        finish,
        out_shape=out_shapes,
        in_specs=[hbm] * 5,
        out_specs=(hbm,) * 5,
        scratch_shapes=[pltpu.VMEM(s.shape, s.dtype) for s in out_shapes] + [dma((5,)), dma((5,))],
        compiler_params=pltpu.CompilerParams(vmem_limit_bytes=VMEM_LIMIT),
        cost_estimate=pl.CostEstimate(
            flops=0, bytes_accessed=6 * DQ * FQ * 4, transcendentals=0
        ),
    )(*results)
    return (layer_out.T, token_grad.T, gate_grad.T[None], up_grad.T[None], down_grad.T[None])


def solution(mesh):
    placed = (
        P("own", None),
        P("own", None),
        P("own", None),
        P("own", None),
        P(("own", "grp"), None, None),
        P(("own", "grp"), None, None),
        P(("own", "grp"), None, None),
    )
    return jax.shard_map(
        on_device,
        mesh=mesh,
        in_specs=placed,
        out_specs=(
            P("own", "grp"),
            P("own", "grp"),
            P(("own", "grp"), None, None),
            P(("own", "grp"), None, None),
            P(("own", "grp"), None, None),
        ),
        check_vma=False,
    )
```

time: 114 us -> 102 us (0.89)
  the two profiles are of different devices: /device:TPU:7 before, /device:TPU:14 now
where the time goes in v2:
time: 102 us
  Pallas kernels  101 us (99%)
    pallas_call x1, Pallas kernels, on_device(): pl.pallas_call(kernel, out_shape=out_shapes, in_specs=[hbm] * 7, out_spec...  98.8 us
    pallas_call x1, Pallas kernels, on_device(): pl.pallas_call(finish, out_shape=out_shapes, in_specs=[hbm] * 5, out_spec...  2.56 us

profile of v2, /device:TPU:14, one launch (start us, length us, event | category | flops | bytes accessed | tf_op | source)
XLA Modules:
  0.0 102.0 jit_solution(11849413761427590897)
XLA Ops:
  0.6 98.8 %shard_map.110 = (bf16[64,128]{1,0:T(8,128)(2,1)}, bf16[64,128]{1,0:T(8,128)(2,1)}, f32[352,512]{1,0:T(8,128)}, f32[352,512]{1,0:T(8,128)}, f32[352,512]{1,0:T(8,128)}) custom-call(s32[6,128]{1,0:T(8,128)} %bitcast.30, f32[6,128]{1,0:T(8,128)} %bitcast.31, bf16[128,2048]{1,0:T(8,128)(2,1)} %tok_hbm.1, bf16[128,2048]{1,0:T(8,128)(2,1)} %cot_hbm.1, ...), custom_call_target="tpu_custom_call" | custom-call | flops 1660944384 | bytes 8388608 | tf_op jit(solution)/shard_map/pallas_call | solution.py:416
  99.4 2.6 %shard_map.111 = (bf16[64,128]{1,0:T(8,128)(2,1)}, bf16[64,128]{1,0:T(8,128)(2,1)}, f32[352,512]{1,0:T(8,128)}, f32[352,512]{1,0:T(8,128)}, f32[352,512]{1,0:T(8,128)}) custom-call(bf16[64,128]{1,0:T(8,128)(2,1)} %get-tuple-element.15.refs_0_, bf16[64,128]{1,0:T(8,128)(2,1)} %get-tuple-element.16.refs_1_, f32[352,512]{1,0:T(8,128)} %get-tuple-element.17.refs_2_, ...), custom_call_target="tpu_custom_call" | custom-call | bytes 4325376 | tf_op jit(solution)/shard_map/pallas_call | solution.py:481

commit v3 on v2

--- a/solution.py
+++ b/solution.py
@@ -55,7 +55,7 @@
     cot,
     wgt,
     sel16,
-    row_w,
+    wsel_ref,
     sel_t,
     whi_t,
     wlo_t,
@@ -89,7 +89,8 @@
     fw_recv,
     r_send,
     r_recv,
-    cx_sem,
+    cx_send,
+    cx_recv,
     bx_send,
     bx_recv,
 ):
@@ -146,7 +147,7 @@
     def _(step):
         greet(dev_own((me + step) % OWN))
 
-    for dev in (dev_above, dev_below, dev_pair, dev_b(1), dev_b(2), dev_b(3)):
+    for dev in (dev_above, dev_below, dev_pair, dev_b(1), dev_b(3)):
         greet(dev)
 
     loads[0].wait()
@@ -161,23 +162,10 @@
     earlier = (iota((TOK, TOK), 0) < iota((TOK, TOK), 1)).astype(F32).astype(BF16)
     place = mm(named.astype(BF16), earlier)
     place = jnp.where(named > 0.5, place, -1.0).astype(BF16)
-    pos_of = iota((ROWS, OWN), 0) // SLOT
-    step_of = pos_of % BPC // 2
-    owner_of = (zl - step_of + 4) % 4 * 8 + (xx + step_of - pos_of // BPC + 8) % 4 * 2 + pos_of % 2
-    spread = (owner_of == iota((ROWS, OWN), 1)).astype(F32).astype(BF16)
-    place_rows = mm(spread, place)
-    taken = place_rows == (iota((ROWS, TOK), 0) % SLOT).astype(F32)
     w1 = weight.astype(BF16)
     rest = weight - w1.astype(F32)
     w2 = rest.astype(BF16)
     w3 = (rest - w2.astype(F32)).astype(BF16)
-    weight_rows = mm(spread, w1) + mm(spread, w2) + mm(spread, w3)
-    sel = jnp.where(taken, 1.0, 0.0)
-    wsel = jnp.where(taken, weight_rows, 0.0)
-    row_weight = jnp.sum(wsel, axis=1, keepdims=True)
-    sel16[...] = sel.astype(BF16)
-    row_w[...] = row_weight
-
     for load in loads[2:4]:
         load.wait()
 
@@ -187,17 +175,27 @@
     def lanes_of(chunk):
         return pl.ds(pl.multiple_of(chunk * CHUNK, CHUNK), CHUNK)
 
-    for order, chunk in enumerate((across, above, below, aa)):
-        picks = sel16[lanes_of(chunk), :]
+    def dispatch(chunk, first=False):
+        pos_of = iota((CHUNK, OWN), 0) // SLOT
+        step_of = pos_of // 2
+        owner_of = (zl - step_of + 4) % 4 * 8 + (xx + step_of - chunk + 8) % 4 * 2 + pos_of % 2
+        spread = (owner_of == iota((CHUNK, OWN), 1)).astype(F32).astype(BF16)
+        taken = mm(spread, place) == (iota((CHUNK, TOK), 0) % SLOT).astype(F32)
+        weight_rows = mm(spread, w1) + mm(spread, w2) + mm(spread, w3)
+        wsel = jnp.where(taken, weight_rows, 0.0)
+        row_weight = jnp.sum(wsel, axis=1, keepdims=True)
+        picks = jnp.where(taken, 1.0, 0.0).astype(BF16)
+        sel16[lanes_of(chunk), :] = picks
+        wsel_ref[lanes_of(chunk), :] = wsel
         x_rows = mm(picks, tok[...])
-        c_rows = row_w[lanes_of(chunk), :] * mm(picks, cot[...])
+        c_rows = row_weight * mm(picks, cot[...])
         send[0, rows_of(chunk)] = x_rows.astype(BF16).reshape(BPC, SLOT, DQ)
         send[1, rows_of(chunk)] = c_rows.astype(BF16).reshape(BPC, SLOT, DQ)
-        if order == 0:
-            pl.semaphore_wait(barrier, OWN - 1 + 6)
+        if first:
+            pl.semaphore_wait(barrier, OWN - 1 + 5)
 
         @pl.loop(0, BPC)
-        def _(step, chunk=chunk):
+        def _(step):
             dl, core2 = step // 2, step % 2
             other = (zl - dl + 4) % 4 * 8 + (xx + dl - chunk + 8) % 4 * 2 + core2
             src = send.at[:, chunk * BPC + step]
@@ -211,11 +209,8 @@
             def _():
                 remote(src, dst, d_send, d_recv.at[chunk], dev_own(other)).start()
 
-    wsel_t = wsel.T
-    hi = wsel_t.astype(BF16)
-    whi_t[...] = hi
-    wlo_t[...] = (wsel_t - hi.astype(F32)).astype(BF16)
-    sel_t[...] = sel.T.astype(BF16)
+    dispatch(across, first=True)
+    dispatch(above)
     for load in loads[4:]:
         load.wait()
 
@@ -249,7 +244,8 @@
             quarter = RELAYED[way][i]
             block = (slice(None), units(quarter))
             go("far", way, quarter, far.at[block], relay.at[block], (far_send, far_recv))
-    for way, chunk in ((UP, above), (DOWN, below)):
+    for way, chunk, later in ((UP, above, below), (DOWN, below, aa)):
+        dispatch(later)
         for t, value in enumerate(partials(chunk)):
             keep[way, t] = value
             near[way, t] = value.astype(BF16)
@@ -267,6 +263,12 @@
             for t, value in enumerate(partials(aa)):
                 mine[t] = value
 
+    wsel_t = wsel_ref[...].T
+    hi = wsel_t.astype(BF16)
+    whi_t[...] = hi
+    wlo_t[...] = (wsel_t - hi.astype(F32)).astype(BF16)
+    sel_t[...] = sel16[...].astype(F32).T.astype(BF16)
+
     def pass_on(kind, way, chunk, quarter, sems):
         block = hid.at[:, units(quarter), lanes_of(chunk)]
         go(kind, way, quarter, block, block, sems)
@@ -330,19 +332,23 @@
             arrived(fw_recv, way, across, quarter)
     give_back(across)
 
-    def combine(chunk):
+    def arrived_home(chunk):
         block = home.at[:, rows_of(chunk)]
         pltpu.make_async_copy(block, block, r_recv.at[chunk]).wait()
+
+    def combine(chunk, some=slice(None)):
         lanes = lanes_of(chunk)
         out_home = home[0, rows_of(chunk)].reshape(CHUNK, DQ)
         grad_home = home[1, rows_of(chunk)].reshape(CHUNK, DQ)
         return (
-            mm(whi_t[:, lanes], out_home) + mm(wlo_t[:, lanes], out_home),
-            mm(sel_t[:, lanes], grad_home),
+            mm(whi_t[some, lanes], out_home) + mm(wlo_t[some, lanes], out_home),
+            mm(sel_t[some, lanes], grad_home),
         )
 
+    arrived_home(aa)
     part[0], part[1] = combine(aa)
     for chunk in (below, above):
+        arrived_home(chunk)
         layer, tgrad = combine(chunk)
         part[0] += layer
         part[1] += tgrad
@@ -350,45 +356,62 @@
     for side, kind, out in ((0, 1, gate_out), (0, 2, up_out), (1, 0, down_out)):
         out[...] = mm(hid[kind], recv[side].reshape(ROWS, DQ))
 
-    layer, tgrad = combine(across)
-    part[0] += layer
-    part[1] += tgrad
-
     kept = pl.ds(pl.multiple_of(cc * 256, 256), 256)
     given = pl.ds(pl.multiple_of((1 - cc) * 256, 256), 256)
-    cx_out[...] = part[:, :, given].astype(BF16)
-    cx = remote(cx_out, cx_in, cx_sem.at[0], cx_sem.at[1], dev_pair)
-    cx.start()
-    cx.wait_recv()
-    total = part[:, :, kept] + cx_in[...].astype(F32)
-    for p in range(4):
-        piece = jnp.concatenate(
-            [total[0, :, 64 * p : 64 * p + 64], total[1, :, 64 * p : 64 * p + 64]], axis=1
-        )
-        pieces[p] = piece
-        bx_out[p] = piece.astype(BF16)
+    halves = (pl.ds(0, TOK // 2), pl.ds(TOK // 2, TOK // 2))
+    arrived_home(across)
+    cx = []
+    for h, some in enumerate(halves):
+        layer, tgrad = combine(across, some)
+        part[0, some] += layer
+        part[1, some] += tgrad
+        cx_out[h] = part[:, some, given].astype(BF16)
+        copy = remote(cx_out.at[h], cx_in.at[h], cx_send.at[h], cx_recv.at[h], dev_pair)
+        copy.start()
+        cx.append(copy)
     bx = []
-    for k in (1, 2, 3):
-        copy = remote(
-            bx_out.at[(bb + k) % 4],
-            bx_in.at[k - 1],
-            bx_send.at[k - 1],
-            bx_recv.at[k - 1],
-            dev_b(k),
-        )
+
+    def hop_to(kind, h, src, dev):
+        index = 3 * h + kind
+        copy = remote(src, bx_in.at[kind, h], bx_send.at[index], bx_recv.at[index], dev)
         copy.start()
         bx.append(copy)
-    final = pieces[bb]
-    for k in range(3):
-        bx[k].wait_recv()
-        final = final + bx_in[k].astype(F32)
+
+    for h, some in enumerate(halves):
+        cx[h].wait_recv()
+        total = part[:, some, kept] + cx_in[h].astype(F32)
+        for p in range(4):
+            piece = jnp.concatenate(
+                [total[0, :, 64 * p : 64 * p + 64], total[1, :, 64 * p : 64 * p + 64]], axis=1
+            )
+            pieces[p, some] = piece
+            bx_out[h, p] = piece.astype(BF16)
+        far_dev, near_dev = (dev_b(1), dev_b(3)) if h == 0 else (dev_b(3), dev_b(1))
+        near_b = (bb + 3) % 4 if h == 0 else (bb + 1) % 4
+        hop_to(0, h, bx_out.at[h, (bb + 2) % 4], far_dev)
+        hop_to(1, h, bx_out.at[h, near_b], near_dev)
+    for h, some in enumerate(halves):
+        bx[2 * h].wait_recv()
+        far_dev = dev_b(1) if h == 0 else dev_b(3)
+        far_b = (bb + 1) % 4 if h == 0 else (bb + 3) % 4
+        bx_out[h, far_b] = (pieces[far_b, some] + bx_in[0, h].astype(F32)).astype(BF16)
+        hop_to(2, h, bx_out.at[h, far_b], far_dev)
+    for index in (1, 3, 4, 5):
+        bx[index].wait_recv()
+    final = jnp.concatenate(
+        [
+            pieces[bb, some] + bx_in[1, h].astype(F32) + bx_in[2, h].astype(F32)
+            for h, some in enumerate(halves)
+        ],
+        axis=0,
+    )
     final = final.T
     layer_ref[...] = final[:64].astype(BF16)
     tgrad_ref[...] = final[64:].astype(BF16)
 
     pltpu.make_async_copy(send.at[:, : OWN - 1], recv.at[:, : OWN - 1], d_send).wait()
     pltpu.make_async_copy(back.at[:, : OWN - 1], home.at[:, : OWN - 1], r_send).wait()
-    for copy in list(copies.values()) + [cx] + bx:
+    for copy in list(copies.values()) + cx + bx:
         copy.wait_send()
 
 
@@ -425,7 +448,7 @@
             pltpu.VMEM((TOK, DQ), BF16),
             pltpu.VMEM((3, FQ, DQ), BF16),
             pltpu.VMEM((ROWS, TOK), BF16),
-            pltpu.VMEM((ROWS, 1), F32),
+            pltpu.VMEM((ROWS, TOK), F32),
             pltpu.VMEM((TOK, ROWS), BF16),
             pltpu.VMEM((TOK, ROWS), BF16),
             pltpu.VMEM((TOK, ROWS), BF16),
@@ -441,11 +464,11 @@
             pltpu.VMEM((2, OWN, SLOT, DQ), BF16),
             pltpu.VMEM((2, OWN, SLOT, DQ), BF16),
             pltpu.VMEM((2, TOK, DQ), F32),
-            pltpu.VMEM((2, TOK, 256), BF16),
-            pltpu.VMEM((2, TOK, 256), BF16),
+            pltpu.VMEM((2, 2, TOK // 2, 256), BF16),
+            pltpu.VMEM((2, 2, TOK // 2, 256), BF16),
             pltpu.VMEM((4, TOK, 128), F32),
-            pltpu.VMEM((4, TOK, 128), BF16),
-            pltpu.VMEM((3, TOK, 128), BF16),
+            pltpu.VMEM((2, 4, TOK // 2, 128), BF16),
+            pltpu.VMEM((3, 2, TOK // 2, 128), BF16),
             dma((7,)),
             dma,
             dma((4,)),
@@ -460,8 +483,9 @@
             dma,
             dma((4,)),
             dma((2,)),
-            dma((3,)),
-            dma((3,)),
+            dma((2,)),
+            dma((6,)),
+            dma((6,)),
         ],
         compiler_params=pltpu.CompilerParams(
             collective_id=0, has_side_effects=True, vmem_limit_bytes=VMEM_LIMIT

time: 102 us -> 98.2 us (0.963)
  the two profiles are of different devices: /device:TPU:14 before, /device:TPU:24 now
where the time goes in v3:
time: 98.2 us; the launch traced here: 98 us
  Pallas kernels  97.4 us (99%)
    pallas_call x1, Pallas kernels, on_device(): pl.pallas_call(kernel, out_shape=out_shapes, in_specs=[hbm] * 7, out_spec...  94.8 us
    pallas_call x1, Pallas kernels, on_device(): pl.pallas_call(finish, out_shape=out_shapes, in_specs=[hbm] * 5, out_spec...  2.56 us

profile of v3, /device:TPU:24, one launch (start us, length us, event | category | flops | bytes accessed | tf_op | source)
XLA Modules:
  0.0 98.0 jit_solution(4180414185278894125)
XLA Ops:
  0.6 94.8 %shard_map.110 = (bf16[64,128]{1,0:T(8,128)(2,1)}, bf16[64,128]{1,0:T(8,128)(2,1)}, f32[352,512]{1,0:T(8,128)}, f32[352,512]{1,0:T(8,128)}, f32[352,512]{1,0:T(8,128)}) custom-call(s32[6,128]{1,0:T(8,128)} %bitcast.30, f32[6,128]{1,0:T(8,128)} %bitcast.31, bf16[128,2048]{1,0:T(8,128)(2,1)} %tok_hbm.1, bf16[128,2048]{1,0:T(8,128)(2,1)} %cot_hbm.1, ...), custom_call_target="tpu_custom_call" | custom-call | flops 1660944384 | bytes 8388608 | tf_op jit(solution)/shard_map/pallas_call | solution.py:439
  95.4 2.6 %shard_map.111 = (bf16[64,128]{1,0:T(8,128)(2,1)}, bf16[64,128]{1,0:T(8,128)(2,1)}, f32[352,512]{1,0:T(8,128)}, f32[352,512]{1,0:T(8,128)}, f32[352,512]{1,0:T(8,128)}) custom-call(bf16[64,128]{1,0:T(8,128)(2,1)} %get-tuple-element.15.refs_0_, bf16[64,128]{1,0:T(8,128)(2,1)} %get-tuple-element.16.refs_1_, f32[352,512]{1,0:T(8,128)} %get-tuple-element.17.refs_2_, ...), custom_call_target="tpu_custom_call" | custom-call | bytes 4325376 | tf_op jit(solution)/shard_map/pallas_call | solution.py:505

commit v4 on v3

--- a/solution.py
+++ b/solution.py
@@ -76,6 +76,7 @@
     pieces,
     bx_out,
     bx_in,
+    grads,
     in_sem,
     d_send,
     d_recv,
@@ -93,6 +94,7 @@
     cx_recv,
     bx_send,
     bx_recv,
+    out_sem,
 ):
     me = lax.axis_index("own")
     grp = lax.axis_index("grp")
@@ -353,8 +355,12 @@
         part[0] += layer
         part[1] += tgrad
 
-    for side, kind, out in ((0, 1, gate_out), (0, 2, up_out), (1, 0, down_out)):
-        out[...] = mm(hid[kind], recv[side].reshape(ROWS, DQ))
+    stores = []
+    for t, (side, kind, out) in enumerate(((0, 1, gate_out), (0, 2, up_out), (1, 0, down_out))):
+        grads[t] = mm(hid[kind], recv[side].reshape(ROWS, DQ))
+        store = pltpu.make_async_copy(grads.at[t], out, out_sem.at[t])
+        store.start()
+        stores.append(store)
 
     kept = pl.ds(pl.multiple_of(cc * 256, 256), 256)
     given = pl.ds(pl.multiple_of((1 - cc) * 256, 256), 256)
@@ -413,6 +419,8 @@
     pltpu.make_async_copy(back.at[:, : OWN - 1], home.at[:, : OWN - 1], r_send).wait()
     for copy in list(copies.values()) + cx + bx:
         copy.wait_send()
+    for store in stores:
+        store.wait()
 
 
 def finish(*refs):
@@ -440,7 +448,7 @@
         kernel,
         out_shape=out_shapes,
         in_specs=[hbm] * 7,
-        out_specs=(vmem,) * 5,
+        out_specs=(vmem, vmem, hbm, hbm, hbm),
         scratch_shapes=[
             pltpu.VMEM((TOP, TOK), jnp.int32),
             pltpu.VMEM((TOP, TOK), F32),
@@ -469,6 +477,7 @@
             pltpu.VMEM((4, TOK, 128), F32),
             pltpu.VMEM((2, 4, TOK // 2, 128), BF16),
             pltpu.VMEM((3, 2, TOK // 2, 128), BF16),
+            pltpu.VMEM((3, FQ, DQ), F32),
             dma((7,)),
             dma,
             dma((4,)),
@@ -486,6 +495,7 @@
             dma((2,)),
             dma((6,)),
             dma((6,)),
+            dma((3,)),
         ],
         compiler_params=pltpu.CompilerParams(
             collective_id=0, has_side_effects=True, vmem_limit_bytes=VMEM_LIMIT

time: 98.2 us -> 97.6 us (level)
  no operation moved by 1% of the time
where the time goes in v4:
time: 97.6 us; the launch traced here: 97.3 us
  Pallas kernels  96.7 us (99%)
    pallas_call x1, Pallas kernels, on_device(): pl.pallas_call(kernel, out_shape=out_shapes, in_specs=[hbm] * 7, out_spec...  94.1 us
    pallas_call x1, Pallas kernels, on_device(): pl.pallas_call(finish, out_shape=out_shapes, in_specs=[hbm] * 5, out_spec...  2.56 us

profile of v4, /device:TPU:24, one launch (start us, length us, event | category | flops | bytes accessed | tf_op | source)
XLA Modules:
  0.0 97.3 jit_solution(11771220186086441166)
XLA Ops:
  0.6 94.1 %shard_map.110 = (bf16[64,128]{1,0:T(8,128)(2,1)}, bf16[64,128]{1,0:T(8,128)(2,1)}, f32[352,512]{1,0:T(8,128)}, f32[352,512]{1,0:T(8,128)}, f32[352,512]{1,0:T(8,128)}) custom-call(s32[6,128]{1,0:T(8,128)} %bitcast.30, f32[6,128]{1,0:T(8,128)} %bitcast.31, bf16[128,2048]{1,0:T(8,128)(2,1)} %tok_hbm.1, bf16[128,2048]{1,0:T(8,128)(2,1)} %cot_hbm.1, ...), custom_call_target="tpu_custom_call" | custom-call | flops 1660944384 | bytes 8388608 | tf_op jit(solution)/shard_map/pallas_call | solution.py:447
  94.8 2.6 %shard_map.111 = (bf16[64,128]{1,0:T(8,128)(2,1)}, bf16[64,128]{1,0:T(8,128)(2,1)}, f32[352,512]{1,0:T(8,128)}, f32[352,512]{1,0:T(8,128)}, f32[352,512]{1,0:T(8,128)}) custom-call(bf16[64,128]{1,0:T(8,128)(2,1)} %get-tuple-element.15.refs_0_, bf16[64,128]{1,0:T(8,128)(2,1)} %get-tuple-element.16.refs_1_, f32[352,512]{1,0:T(8,128)} %get-tuple-element.17.refs_2_, ...), custom_call_target="tpu_custom_call" | custom-call | bytes 4325376 | tf_op jit(solution)/shard_map/pallas_call | solution.py:515

commit v5 on v4

--- a/solution.py
+++ b/solution.py
@@ -177,7 +177,7 @@
     def lanes_of(chunk):
         return pl.ds(pl.multiple_of(chunk * CHUNK, CHUNK), CHUNK)
 
-    def dispatch(chunk, first=False):
+    def select(chunk):
         pos_of = iota((CHUNK, OWN), 0) // SLOT
         step_of = pos_of // 2
         owner_of = (zl - step_of + 4) % 4 * 8 + (xx + step_of - chunk + 8) % 4 * 2 + pos_of % 2
@@ -193,9 +193,8 @@
         c_rows = row_weight * mm(picks, cot[...])
         send[0, rows_of(chunk)] = x_rows.astype(BF16).reshape(BPC, SLOT, DQ)
         send[1, rows_of(chunk)] = c_rows.astype(BF16).reshape(BPC, SLOT, DQ)
-        if first:
-            pl.semaphore_wait(barrier, OWN - 1 + 5)
-
+
+    def dispatch(chunk):
         @pl.loop(0, BPC)
         def _(step):
             dl, core2 = step // 2, step % 2
@@ -211,8 +210,13 @@
             def _():
                 remote(src, dst, d_send, d_recv.at[chunk], dev_own(other)).start()
 
-    dispatch(across, first=True)
+    select(across)
+    pl.semaphore_wait(barrier, OWN - 1 + 5)
+    dispatch(across)
+    select(above)
     dispatch(above)
+    select(below)
+    select(aa)
     for load in loads[4:]:
         load.wait()
 

time: 97.6 us -> 97.5 us (level)
  no operation moved by 1% of the time
where the time goes in v5:
time: 97.5 us; the launch traced here: 97.3 us
  Pallas kernels  96.7 us (99%)
    pallas_call x1, Pallas kernels, on_device(): pl.pallas_call(kernel, out_shape=out_shapes, in_specs=[hbm] * 7, out_spec...  94.1 us
    pallas_call x1, Pallas kernels, on_device(): pl.pallas_call(finish, out_shape=out_shapes, in_specs=[hbm] * 5, out_spec...  2.56 us

profile of v5, /device:TPU:24, one launch (start us, length us, event | category | flops | bytes accessed | tf_op | source)
XLA Modules:
  0.0 97.3 jit_solution(1663870524655668720)
XLA Ops:
  0.6 94.1 %shard_map.110 = (bf16[64,128]{1,0:T(8,128)(2,1)}, bf16[64,128]{1,0:T(8,128)(2,1)}, f32[352,512]{1,0:T(8,128)}, f32[352,512]{1,0:T(8,128)}, f32[352,512]{1,0:T(8,128)}) custom-call(s32[6,128]{1,0:T(8,128)} %bitcast.30, f32[6,128]{1,0:T(8,128)} %bitcast.31, bf16[128,2048]{1,0:T(8,128)(2,1)} %tok_hbm.1, bf16[128,2048]{1,0:T(8,128)(2,1)} %cot_hbm.1, ...), custom_call_target="tpu_custom_call" | custom-call | flops 1660944384 | bytes 8388608 | tf_op jit(solution)/shard_map/pallas_call | solution.py:451
  94.7 2.6 %shard_map.111 = (bf16[64,128]{1,0:T(8,128)(2,1)}, bf16[64,128]{1,0:T(8,128)(2,1)}, f32[352,512]{1,0:T(8,128)}, f32[352,512]{1,0:T(8,128)}, f32[352,512]{1,0:T(8,128)}) custom-call(bf16[64,128]{1,0:T(8,128)(2,1)} %get-tuple-element.15.refs_0_, bf16[64,128]{1,0:T(8,128)(2,1)} %get-tuple-element.16.refs_1_, f32[352,512]{1,0:T(8,128)} %get-tuple-element.17.refs_2_, ...), custom_call_target="tpu_custom_call" | custom-call | bytes 4325376 | tf_op jit(solution)/shard_map/pallas_call | solution.py:519
